TPU v7x, 128 devices: a whole 4x4x4 slice. The times are simulated.
128 devices in a mesh: grp: 2 (over z_hi), dp: 64 (over z_lo, y, x, core).
Axes of the slice: x: 4, y: 4, z: 4 (z_hi: 2, z_lo: 2; z = z_hi * 2 + z_lo), core: 2. Of those that a mesh axis runs over, the one named last changes fastest.
Arguments:
- teacher_hidden: bfloat16 [256, 256, 1024], P(('grp', 'dp')), may hold values from -6 to 6
- passage_len: int32 [256], P(('grp', 'dp')), may hold values from 56 to 224
- qkv_weight: bfloat16 [1024, 3072], P('dp'), may hold values from -0.1875 to 0.1875
- out_weight: bfloat16 [1024, 1024], P(None, 'dp'), may hold values from -0.1875 to 0.1875
- teacher_gain: float32 [1024], replicated, may hold values from 0.25 to 1.75
- score_weight: float32 [1024], replicated, may hold values from -0.375 to 0.375
- query_tokens: bfloat16 [8, 32, 768], replicated, may hold values from -6 to 6
- passage_tokens: bfloat16 [256, 224, 768], P(('grp', 'dp')), may hold values from -6 to 6
- w_in: bfloat16 [768, 3072], replicated, may hold values from -0.21875 to 0.21875
- w_out: bfloat16 [3072, 768], replicated, may hold values from -0.109375 to 0.109375
Outputs:
- teacher_scores: float32 [256], P(('grp', 'dp'))
- grad_in: float32 [768, 3072], P(('grp', 'dp'))
- grad_out: float32 [3072, 768], P(('grp', 'dp'))
All inputs are finite; a program needn't handle non-finite values.
Results may differ from a plain program's by a relative error of at most 0.027.
Values may be sent and summed in bfloat16 or wider, within the bound.
No kernel may reach another device: no remote copies, remote signals or barrier semaphores. Data moves between devices by JAX's collectives and lax.ppermute only.
A program may use at most 128 MiB of HBM per device.

v0:
```python
import jax
import jax.numpy as jnp
from jax import lax
from jax.experimental import pallas as pl
from jax.experimental.pallas import tpu as pltpu
from jax.sharding import Mesh
from jax.sharding import PartitionSpec as P

HD = 64
SQ = 32
SP = 224
S = SQ + SP
DT = 1024
DS = 768
FF = 3072
CHIPS = 64
QUARTER = 4 * HD
WIDE = 3 * DS
PAY = WIDE + 128 + DS // 2
EPS = 1e-05
LOSS_SCALE = 8.0
MIB = 1 << 20

AXES = ("zh", "zl", "y", "xh", "xl", "c")
DP = ("zl", "y", "xh", "xl", "c")
X = ("xh", "xl")
CHIP_AXES = ("zh", "zl", "y", "xh", "xl")
RIVALS = ("zh", "y", "xh")
SWAP = [(0, 1), (1, 0)]
BOTH = [(0, 3), (1, 2), (2, 1), (3, 0)]

F32 = jnp.float32
BF16 = jnp.bfloat16
NT = (((1,), (1,)), ((), ()))


def params(mib):
    return pltpu.CompilerParams(vmem_limit_bytes=mib * MIB)


def ring(step):
    return [(i, (i + step) % 4) for i in range(4)]


def mm(a, b):
    return jnp.dot(a, b, preferred_element_type=F32)


def mm_nt(a, b):
    return lax.dot_general(a, b, NT, preferred_element_type=F32)


def iota(shape, dim):
    return lax.broadcasted_iota(jnp.int32, shape, dim)


def send_axis(piece, axis):
    return [piece] + [lax.ppermute(piece, axis, ring(step)) for step in (1, 3, 2)]


def join_axis(pieces, axis, dim):
    here, piece = lax.axis_index(axis), pieces[0]
    shape = piece.shape[:dim] + (4,) + piece.shape[dim + 1 :]
    whole = jnp.zeros(shape, piece.dtype)
    for part, step in zip(pieces, (0, 1, 3, 2)):
        start = [0] * len(shape)
        start[dim] = (here - step) % 4
        whole = lax.dynamic_update_slice(whole, part, tuple(start))
    return whole


def student_kernel(
    lens, half_ref, first_ref, q_ref, p_ref, win_hbm, wout_hbm, sums_tiles, score_ref, g_ref, gp_hbm, other_hbm,
    rows, win, wout, slope, pulled_ref, sums_ref, gp, blocks, in_sems, out_sems, wout_sem, other_sems,
):
    def load(j):
        cols = pl.ds(pl.multiple_of(j * 512, 512), 512)
        return pltpu.make_async_copy(win_hbm.at[:, cols], win.at[:, cols], in_sems.at[j])

    def save(j):
        cols = pl.ds(pl.multiple_of(j * DS, DS), DS)
        return pltpu.make_async_copy(gp.at[:, :, cols], gp_hbm.at[:, :, cols], out_sems.at[j])

    def send(i, k):
        cols = pl.ds(k * DS, DS)
        return pltpu.make_async_copy(
            blocks.at[i, :, cols], other_hbm.at[i, :, cols], other_sems.at[i * 3 + k]
        )

    load_out = pltpu.make_async_copy(wout_hbm, wout, wout_sem)
    for j in range(6):
        load(j).start()
    load_out.start()
    for i in range(2):
        rows[i * S : i * S + SQ] = q_ref[first_ref[0] + i]
        rows[i * S + SQ : (i + 1) * S] = p_ref[i]
    at_row = iota((S, 1), 0) - SQ

    def pool(values):
        sums = []
        for i in range(2):
            part = values[i * S : (i + 1) * S].astype(F32)
            sums.append(jnp.sum(part[:SQ], 0, keepdims=True))
            part = jnp.where(at_row[SQ:] < lens[i], part[SQ:], 0.0)
            sums.append(jnp.sum(part, 0, keepdims=True))
        return jnp.concatenate(sums + sums, 0)


    def forward(j, carry):
        load(j).wait()
        for part in range(2):
            cols = pl.ds(pl.multiple_of(j * 512 + part * 256, 256), 256)
            pre = mm(rows[...], win[:, cols])
            bell = jnp.exp2(pre * pre * -0.7213475204444817)
            denominator = 1.0 + jnp.abs(pre) * (0.3275911 * 0.7071067811865476)
            t = pl.reciprocal(denominator, approx=True)
            t = t * (2.0 - denominator * t)
            poly = 0.5 * 1.061405429 * t - 0.5 * 1.453152027
            poly = poly * t + 0.5 * 1.421413741
            poly = poly * t - 0.5 * 0.284496736
            poly = poly * t + 0.5 * 0.254829592
            tail = poly * t * bell
            cdf = jnp.where(pre < 0.0, tail, 1.0 - tail)
            slope[:, cols] = cdf + pre * bell * 0.3989422804014327
            sums_ref[:, cols] = pool(pre * cdf)
        return carry

    lax.fori_loop(0, FF // 512, forward, 0)
    load_out.wait()
    sums = sums_ref[...]
    high = sums.astype(BF16)
    low = (sums - high.astype(F32)).astype(BF16)
    out = mm(jnp.concatenate([high, low], 0), wout[...])
    row8 = iota((8, 1), 0)
    count = jnp.where(row8 % 2 == 0, SQ, jnp.where(row8 < 2, lens[0], lens[1])).astype(F32)
    means = (pool(rows[...]) + out[:8] + out[8:]) / count
    means = means[:4]
    centred = means - jnp.mean(means, -1, keepdims=True)
    scale = lax.rsqrt(jnp.mean(centred * centred, -1, keepdims=True) + EPS)
    unit = centred * scale
    other = jnp.concatenate([unit[1:2], unit[0:1], unit[3:4], unit[2:3]], 0)
    cross = jnp.sum(unit * other, -1, keepdims=True) * DS ** (-0.5)
    back = other * DS ** (-0.5)
    back = scale * (
        back
        - jnp.mean(back, -1, keepdims=True)
        - unit * jnp.mean(back * unit, -1, keepdims=True)
    )
    grad = (back / count[:4]).astype(BF16)
    g_ref[...] = grad
    pairs = jnp.concatenate([cross[0:1], cross[2:3]], 0)
    score_ref[...] = jnp.broadcast_to(jnp.concatenate([pairs] * 4, 0), (8, 128))
    grad8 = jnp.concatenate([grad, jnp.zeros((4, DS), BF16)], 0)
    pulled_ref[...] = mm_nt(grad8, wout[...])
    def backward(j, carry):
        for part in range(3):
            cols = pl.ds(pl.multiple_of(j * DS + part * 256, 256), 256)
            pulled = pulled_ref[:, cols]
            for i in range(2):
                gate = jnp.where(at_row < lens[i], pulled[2 * i + 1 : 2 * i + 2], 0.0)
                gp[i, SQ:, cols] = (gate[SQ:] * slope[i * S + SQ : (i + 1) * S, cols]).astype(BF16)
                gp[i, :SQ, cols] = (
                    pulled[2 * i : 2 * i + 1] * slope[i * S : i * S + SQ, cols]
                ).astype(BF16)
        save(j).start()
        return carry

    lax.fori_loop(0, FF // DS, backward, 0)
    fill = jnp.zeros((4, 16), F32)
    for d in range(CHIPS):
        part = sums[:4, d * 48 : d * 48 + 48]
        sums_tiles[d] = jnp.concatenate([part, fill, part, fill], 1)
    grad_blocks(
        half_ref[0], rows, gp, blocks, lambda i, k: send(i, k).start()
    )
    for j in range(FF // DS):
        save(j).wait()
    for j in range(6):
        send(j // 3, j % 3).wait()


def student(lens, half, first, queries, passages, w_in, w_out):
    vmem = pl.BlockSpec(memory_space=pltpu.VMEM)
    anywhere = pl.BlockSpec(memory_space=pl.ANY)
    return pl.pallas_call(
        student_kernel,
        out_shape=(
            jax.ShapeDtypeStruct((CHIPS, 4, 128), F32),
            jax.ShapeDtypeStruct((8, 128), F32),
            jax.ShapeDtypeStruct((4, DS), BF16),
            jax.ShapeDtypeStruct((2, S, FF), BF16),
            jax.ShapeDtypeStruct((2, 8 * CHIPS, WIDE), BF16),
        ),
        in_specs=[pl.BlockSpec(memory_space=pltpu.SMEM)] * 3 + [vmem, vmem, anywhere, anywhere],
        out_specs=(vmem, vmem, vmem, anywhere, anywhere),
        scratch_shapes=[
            pltpu.VMEM((2 * S, DS), BF16),
            pltpu.VMEM((DS, FF), BF16),
            pltpu.VMEM((FF, DS), BF16),
            pltpu.VMEM((2 * S, FF), F32),
            pltpu.VMEM((8, FF), F32),
            pltpu.VMEM((8, FF), F32),
            pltpu.VMEM((2, S, FF), BF16),
            pltpu.VMEM((2, 8 * CHIPS, WIDE), BF16),
            pltpu.SemaphoreType.DMA((6,)),
            pltpu.SemaphoreType.DMA((4,)),
            pltpu.SemaphoreType.DMA,
            pltpu.SemaphoreType.DMA((6,)),
        ],
        compiler_params=params(60),
        cost_estimate=pl.CostEstimate(flops=1, bytes_accessed=1, transcendentals=0),
        name="student",
    )(lens, half.reshape(1), first.reshape(1), queries, passages, w_in, w_out)


def select_features(half, rows):
    line, feature = iota((8 * CHIPS, DS), 0), iota((8 * CHIPS, DS), 1)
    lane = line % 8
    wanted = jnp.where(lane < 6, (2 * (line // 8) + half) * 6 + lane, -1)
    return mm_nt(jnp.where(feature == wanted, 1.0, 0.0).astype(BF16), rows)


def late_features(wide, k):
    lane = iota((8 * CHIPS, S), 0) % 8
    return jnp.where(
        lane == 6,
        pltpu.roll(wide, 6 - k, 0),
        jnp.where(lane == 7, pltpu.roll(wide, 4 - k, 0), 0.0),
    ).astype(BF16)


def grad_blocks(half, rows, grad, out, done):
    for i in range(2):
        wide = select_features(half, rows[i * S : (i + 1) * S])
        main = wide.astype(BF16)
        for k in range(3):
            rest = late_features(wide, k)
            for part in range(3):
                at = k * DS + part * 256
                late = 3 * DS + part * 256
                out[i, :, at : at + 256] = (
                    mm(main, grad[i, :, at : at + 256]) + mm(rest, grad[i, :, late : late + 256])
                ).astype(BF16)
            done(i, k)


def first_kernel(half_ref, first_ref, q_ref, p_ref, gp_hbm, out_hbm, gp, out, gp_sems, out_sems):
    def block(ref, k):
        return ref.at[:, pl.ds(k * DS, DS)]

    def load(k):
        return pltpu.make_async_copy(block(gp_hbm.at[0], k), block(gp, k), gp_sems.at[k])

    def save(k):
        return pltpu.make_async_copy(block(out, k), block(out_hbm, k), out_sems.at[k])

    for k in (3, 0, 1, 2):
        load(k).start()
    wide = select_features(half_ref[0], jnp.concatenate([q_ref[first_ref[0]], p_ref[0]], 0))
    main = wide.astype(BF16)
    load(3).wait()
    for k in range(3):
        rest = late_features(wide, k)
        load(k).wait()
        for part in range(3):
            cols = slice(k * DS + part * 256, k * DS + part * 256 + 256)
            late = slice(3 * DS + part * 256, 3 * DS + part * 256 + 256)
            out[:, cols] = (mm(main, gp[:, cols]) + mm(rest, gp[:, late])).astype(BF16)
        save(k).start()
    for k in range(3):
        save(k).wait()


def first_term(half, first, queries, passages, grad_pre):
    vmem = pl.BlockSpec(memory_space=pltpu.VMEM)
    anywhere = pl.BlockSpec(memory_space=pl.ANY)
    return pl.pallas_call(
        first_kernel,
        out_shape=jax.ShapeDtypeStruct((8 * CHIPS, WIDE), BF16),
        in_specs=[pl.BlockSpec(memory_space=pltpu.SMEM)] * 2 + [vmem, vmem, anywhere],
        out_specs=anywhere,
        scratch_shapes=[
            pltpu.VMEM((S, FF), BF16),
            pltpu.VMEM((8 * CHIPS, WIDE), BF16),
            pltpu.SemaphoreType.DMA((4,)),
            pltpu.SemaphoreType.DMA((3,)),
        ],
        compiler_params=params(60),
        cost_estimate=pl.CostEstimate(flops=3 * 10**9, bytes_accessed=4 * 10**6, transcendentals=0),
        name="first_term",
    )(half.reshape(1), first.reshape(1), queries, passages, grad_pre)


def turn(values, shift):
    wide = values.shape[1] // 2
    amount = shift * 128
    return jnp.concatenate(
        [pltpu.roll(values[:, :wide], amount, 1), pltpu.roll(values[:, wide:], amount, 1)], 1
    )


def teacher_kernel(
    y_ref, x0, x1, x2, x3, w0, w1, w2, w3, student_ref, near_ref, flip_ref, far_ref, farflip_ref,
    hidden, weight, starts, x_sems, w_sems, sems,
):
    copies, heads = [], []
    for i, ref in enumerate((w0, w1, w2, w3)):
        copies.append(pltpu.make_async_copy(ref, weight.at[i], w_sems.at[i]))
    for i, ref in enumerate((x0, x1, x2, x3)):
        for j in range(2):
            heads.append(
                pltpu.make_async_copy(ref.at[pl.ds(j * S, 16)], starts.at[i, j], sems.at[i, j])
            )
        copies.append(pltpu.make_async_copy(ref, hidden.at[i], x_sems.at[i]))
    for copy in heads + copies:
        copy.start()
    xs, ws = [hidden.at[i] for i in range(4)], [weight.at[i] for i in range(4)]
    there, back = (4 - y_ref[0]) % 4, y_ref[0]
    blocks = [(ws[m], z, (z * 4 + m) * 128) for z in range(2) for m in range(4)]

    def reduce(values, first):
        total = None
        for ref, z, at in blocks:
            term = mm(values[:, at : at + 128], ref[z, :, first : first + QUARTER])
            total = term if total is None else total + term
        return total

    def expand(values, first):
        return jnp.concatenate(
            [mm_nt(values, ref[z, :, first : first + QUARTER]) for ref, z, _ in blocks], 1
        )

    for copy in heads + copies[:4]:
        copy.wait()
    lead = jnp.concatenate([starts[i, j, :1] for i in range(4) for j in range(2)], 0).astype(F32)
    query = reduce(turn(lead, there).astype(BF16), 0).astype(BF16).astype(F32)
    head, col = iota((32, QUARTER), 0) // 8, iota((32, QUARTER), 1) // HD
    spread = jnp.where(head == col, jnp.concatenate([query] * 4, 0), 0.0).astype(BF16)
    keyed = turn(expand(spread, QUARTER), back).astype(BF16)
    logits = []
    for copy, x in zip(copies[4:], xs):
        copy.wait()
        logits.append(mm_nt(keyed, x[: 2 * S]))
    logits = jnp.concatenate(logits, 1) * HD ** (-0.5)
    live = jnp.concatenate([x[2 * S : 2 * S + 1, : 2 * S].astype(F32) for x in xs], 1)
    pair, slot = iota((32, 8 * S), 0) % 8, iota((32, 8 * S), 1) // S
    logits = jnp.where((pair == slot) & (live > 0.5), logits, -1e30)
    weights = jnp.exp(logits - jnp.max(logits, -1, keepdims=True))
    weights = (weights / jnp.sum(weights, -1, keepdims=True)).astype(BF16)
    mixed = mm(weights[:, : 2 * S], xs[0][: 2 * S])
    for i in range(1, 4):
        mixed += mm(weights[:, i * 2 * S : (i + 1) * 2 * S], xs[i][: 2 * S])
    context = reduce(turn(mixed, there).astype(BF16), 2 * QUARTER)
    context = jnp.where(head == col, context, 0.0)
    context = (context[:8] + context[8:16] + context[16:24] + context[24:]).astype(BF16)
    projected = turn(expand(context, 3 * QUARTER), back)
    own = projected[:2] + lead[:2]
    core, far, both = projected[2:4], projected[4:6], projected[6:]
    for ref, order in (
        (near_ref, (own, core, far, both)),
        (flip_ref, (core, own, both, far)),
        (far_ref, (far, both, own, core)),
        (farflip_ref, (both, far, core, own)),
    ):
        ref[:, :DT] = jnp.concatenate(order, 0)
        ref[:, DT:] = student_ref[...]


def teacher_partial(y, xs, ws, student_scores):
    shape = jax.ShapeDtypeStruct((8, DT + 128), F32)
    vmem = pl.BlockSpec(memory_space=pltpu.VMEM)
    return pl.pallas_call(
        teacher_kernel,
        out_shape=(shape,) * 4,
        in_specs=[pl.BlockSpec(memory_space=pltpu.SMEM)]
        + [pl.BlockSpec(memory_space=pl.ANY)] * 8
        + [vmem],
        out_specs=(vmem,) * 4,
        scratch_shapes=[
            pltpu.VMEM((4, 2 * S + 16, DT), BF16),
            pltpu.VMEM((4, 2, 128, DT), BF16),
            pltpu.VMEM((4, 2, 16, DT), BF16),
            pltpu.SemaphoreType.DMA((4,)),
            pltpu.SemaphoreType.DMA((4,)),
            pltpu.SemaphoreType.DMA((4, 2)),
        ],
        compiler_params=params(24),
        cost_estimate=pl.CostEstimate(flops=10**9, bytes_accessed=6 * 10**6, transcendentals=0),
        name="teacher_partial",
    )(y.reshape(1), *xs, *ws, student_scores)


def score_kernel(own, core, far, both, gain, weight, tile_ref, spread_ref, score_ref):
    refs = (own, core, far, both)
    values = own[:, :DT] + core[:, :DT] + far[:, :DT] + both[:, :DT]
    centred = values - jnp.mean(values, -1, keepdims=True)
    unit = centred * lax.rsqrt(jnp.mean(centred * centred, -1, keepdims=True) + EPS)
    score = jnp.sum(unit * gain[...] * weight[...], -1, keepdims=True)
    student = jnp.concatenate([ref[:2, DT:] for ref in refs], 0)
    tile = jnp.where(iota((8, 128), 1) < 64, score, student)
    tile_ref[...] = tile
    for i in range(2):
        score_ref[i] = jnp.sum(score[i : i + 1])
    for i in range(16):
        spread_ref[i] = tile


def score_tile(parts, gain, weight):
    vmem = pl.BlockSpec(memory_space=pltpu.VMEM)
    return pl.pallas_call(
        score_kernel,
        out_shape=(
            jax.ShapeDtypeStruct((8, 128), F32),
            jax.ShapeDtypeStruct((16, 8, 128), F32),
            jax.ShapeDtypeStruct((2,), F32),
        ),
        in_specs=[vmem] * 6,
        out_specs=(vmem, vmem, pl.BlockSpec(memory_space=pltpu.SMEM)),
        compiler_params=params(8),
        name="score_tile",
    )(*parts, gain, weight)


def payload_kernel(
    half_ref, first_ref, tile_ref, all_ref, q_ref, p_ref, gp_hbm, first_hbm, recv_hbm, sums_ref, g_ref, out_hbm,
    gp, term, recv, out, gp_sems, term_sems, recv_sems, out_sems,
):
    def load_grad(k):
        cols = pl.ds(k * DS, DS)
        return pltpu.make_async_copy(gp_hbm.at[1, :, cols], gp.at[:, cols], gp_sems.at[k])

    def load_first(k):
        cols = pl.ds(k * DS, DS)
        return pltpu.make_async_copy(first_hbm.at[:, cols], term.at[:, cols], term_sems.at[k])

    def load_term(k):
        cols = pl.ds(k * DS, DS)
        return pltpu.make_async_copy(recv_hbm.at[:, :, cols], recv.at[:, :, cols], recv_sems.at[k])

    def save(k):
        cols = pl.ds(k * DS, DS) if k < 3 else pl.ds(WIDE, PAY - WIDE)
        return pltpu.make_async_copy(out.at[:, cols], out_hbm.at[:, cols], out_sems.at[k])

    load_grad(3).start()
    for k in range(3):
        load_grad(k).start()
        load_first(k).start()
        load_term(k).start()
    every = jnp.concatenate([all_ref[:, :4], all_ref[:, 4:]], 0)
    top = jnp.max(every, 0)
    lse = top + jnp.log(jnp.sum(jnp.exp(every - top[None]), 0))
    share = jnp.exp(tile_ref[:4] - lse)
    cot = LOSS_SCALE * (share[:, 64:65] - share[:, :1])
    rows = jnp.concatenate([q_ref[first_ref[0] + 1], p_ref[1]], 0)
    wide = select_features(half_ref[0], rows) * cot[1:2]
    main = wide.astype(BF16)
    by_group = jnp.concatenate([cot[j : j + 1] for j in range(2) for _ in range(2)], 0)
    scaled = sums_ref[...] * by_group[None]
    high = scaled.astype(BF16).astype(F32)
    scaled = jnp.where(iota((CHIPS, 4, 128), 2) < 64, high, scaled - high)
    scaled = jnp.concatenate([scaled, scaled], 1).reshape(8 * CHIPS, 128)
    out[:, WIDE : WIDE + 128] = scaled.astype(BF16)
    grad = g_ref[...].astype(F32)
    grad = jnp.concatenate([grad[:, : DS // 2], grad[:, DS // 2 :]], 0)
    out[:, WIDE + 128 :] = jnp.concatenate([grad] * CHIPS, 0).astype(BF16)
    save(3).start()
    load_grad(3).wait()
    for k in range(3):
        rest = late_features(wide, k)
        load_grad(k).wait()
        load_first(k).wait()
        load_term(k).wait()
        for part in range(3):
            cols = slice(k * DS + part * 256, k * DS + part * 256 + 256)
            late = slice(3 * DS + part * 256, 3 * DS + part * 256 + 256)
            total = mm(main, gp[:, cols]) + mm(rest, gp[:, late])
            total += term[:, cols].astype(F32) * cot[:1]
            for i in range(2):
                total += recv[i, :, cols].astype(F32) * cot[2 + i : 3 + i]
            out[:, cols] = total.astype(BF16)
        save(k).start()
    for k in range(4):
        save(k).wait()


def payload(half, first, tile, every, queries, passages, grad_pre, term, received, sums, grad):
    vmem = pl.BlockSpec(memory_space=pltpu.VMEM)
    anywhere = pl.BlockSpec(memory_space=pl.ANY)
    return pl.pallas_call(
        payload_kernel,
        out_shape=jax.ShapeDtypeStruct((CHIPS * 8, PAY), BF16),
        in_specs=[pl.BlockSpec(memory_space=pltpu.SMEM)] * 2
        + [vmem] * 4
        + [anywhere, anywhere, anywhere, vmem, vmem],
        out_specs=anywhere,
        scratch_shapes=[
            pltpu.VMEM((S, FF), BF16),
            pltpu.VMEM((8 * CHIPS, WIDE), BF16),
            pltpu.VMEM((2, 8 * CHIPS, WIDE), BF16),
            pltpu.VMEM((8 * CHIPS, PAY), BF16),
            pltpu.SemaphoreType.DMA((4,)),
            pltpu.SemaphoreType.DMA((3,)),
            pltpu.SemaphoreType.DMA((3,)),
            pltpu.SemaphoreType.DMA((4,)),
        ],
        compiler_params=params(60),
        name="payload",
    )(
        half.reshape(1), first.reshape(1), tile, every, queries, passages, grad_pre, term, received,
        sums, grad,
    )


def sum_kernel(in_ref, gin_ref):
    total = in_ref[0, :, :WIDE].astype(F32)
    for d in range(1, CHIPS):
        total += in_ref[d, :, :WIDE].astype(F32)
    gin_ref[:, :WIDE] = total[:6]
    for r in range(6):
        line, at = 6 + r // 3, r % 3 * DS
        gin_ref[r : r + 1, WIDE:] = total[line : line + 1, at : at + DS]


def sum_terms(incoming):
    vmem = pl.BlockSpec(memory_space=pltpu.VMEM)
    return pl.pallas_call(
        sum_kernel,
        out_shape=jax.ShapeDtypeStruct((6, FF), F32),
        in_specs=[vmem],
        out_specs=vmem,
        compiler_params=params(32),
        name="sum_terms",
    )(incoming)


def outer_kernel(core_ref, in_ref, own_ref, send_ref):
    columns = in_ref[:, :, WIDE : WIDE + 128].astype(F32).reshape(CHIPS * 8, 128).T
    line = iota((128, CHIPS * 8), 1) % 8
    grads = in_ref[:, :, WIDE + 128 :].astype(F32).reshape(CHIPS * 8, DS // 2).astype(BF16)
    left = mm(jnp.where(line < 4, columns, 0.0).astype(BF16), grads)
    right = mm(jnp.where(line < 4, 0.0, columns).astype(BF16), grads)
    both = jnp.concatenate([left[:48] + left[64:112], right[:48] + right[64:112]], 1)
    first = core_ref[0] == 0
    own_ref[...] = jnp.where(first, both[:24], both[24:])
    send_ref[...] = jnp.where(first, both[24:], both[:24])


def outer_terms(core, incoming):
    vmem = pl.BlockSpec(memory_space=pltpu.VMEM)
    part = jax.ShapeDtypeStruct((24, DS), F32)
    return pl.pallas_call(
        outer_kernel,
        out_shape=(part, part),
        in_specs=[pl.BlockSpec(memory_space=pltpu.SMEM), vmem],
        out_specs=(vmem,) * 2,
        compiler_params=params(32),
        name="outer_terms",
    )(core.reshape(1), incoming)


def pack_kernel(me_ref, qkv_ref, out_ref, p0, p1, p2, p3):
    for flip, ref in enumerate((p0, p1, p2, p3)):
        for j in range(4):

            @pl.when(me_ref[0] == j)
            def _():
                who = j ^ flip
                for t in range(3):
                    at = t * DT + who * QUARTER
                    ref[0, :, t * QUARTER : (t + 1) * QUARTER] = qkv_ref[:, at : at + QUARTER]
                ref[0, :, 3 * QUARTER :] = out_ref[:, who * QUARTER : (who + 1) * QUARTER]


def pack_weights(me, qkv_weight, out_weight):
    vmem = pl.BlockSpec(memory_space=pltpu.VMEM)
    return pl.pallas_call(
        pack_kernel,
        out_shape=(jax.ShapeDtypeStruct((1, 16, DT), BF16),) * 4,
        in_specs=[pl.BlockSpec(memory_space=pltpu.SMEM), vmem, vmem],
        out_specs=(vmem,) * 4,
        compiler_params=params(8),
        name="pack_weights",
    )(me.reshape(1), qkv_weight, out_weight.T)


def exchange_weights(qkv_weight, out_weight):
    me = 2 * lax.axis_index("zl") + lax.axis_index("c")
    mine, to_core, to_far, to_both = pack_weights(me, qkv_weight, out_weight)
    from_core = lax.ppermute(to_core, "c", SWAP)
    from_far = lax.ppermute(to_far, "zl", SWAP)
    from_both = lax.ppermute(to_both, ("zl", "c"), BOTH)
    four = jnp.zeros((4, 16, DT), BF16)
    for part, who in ((mine, me), (from_core, me ^ 1), (from_far, me ^ 2), (from_both, me ^ 3)):
        four = lax.dynamic_update_slice(four, part, (who, 0, 0))
    return four.reshape(2, 1, 1, 32, DT)


def body(
    teacher_hidden,
    passage_len,
    qkv_weight,
    out_weight,
    teacher_gain,
    score_weight,
    query_tokens,
    passage_tokens,
    w_in,
    w_out,
):
    core = lax.axis_index("c")
    first = lax.axis_index("xl") * 4 + core * 2

    slots = jnp.arange(S)
    live = (slots[None, :] < SQ) | (slots[None, :] - SQ < passage_len[:, None])
    live = jnp.pad(live.astype(BF16).reshape(1, 2 * S), ((0, 15), (0, DT - 2 * S)))
    hidden = jnp.concatenate([teacher_hidden.reshape(2 * S, DT), live], 0)

    four = exchange_weights(qkv_weight, out_weight)
    four, hidden = lax.optimization_barrier((four, hidden))
    hidden_far = lax.ppermute(hidden, "zl", SWAP)
    hidden_core = lax.ppermute(hidden, "c", SWAP)
    plane = join_axis(send_axis(four, X), X, 2)
    plane, early_query, hidden_core = lax.optimization_barrier((plane, query_tokens, hidden_core))
    planes = send_axis(plane, "y")

    sums, student_scores, grad, grad_pre, other = student(
        passage_len, 1 - core, first, early_query, passage_tokens, w_in, w_out
    )

    planes, other, hidden_far = lax.optimization_barrier((planes, other, hidden_far))
    hidden_both = lax.ppermute(hidden_far, "c", SWAP)
    here, before, after, across = [part.reshape(2, 128, DT) for part in planes]
    near, flip, far, farflip = teacher_partial(
        lax.axis_index("y"),
        (hidden, hidden_core, hidden_far, hidden_both),
        (here, after, across, before),
        student_scores,
    )
    parts = (
        near,
        lax.ppermute(flip, "c", SWAP),
        lax.ppermute(far, "zl", SWAP),
        lax.ppermute(farflip, ("zl", "c"), BOTH),
    )
    tile, spread, scores = score_tile(parts, teacher_gain[None], score_weight[None])
    every = lax.all_to_all(spread, RIVALS, 0, 0, tiled=True)
    other, late_query, _ = lax.optimization_barrier((other, query_tokens, tile))
    received = lax.ppermute(other, "c", SWAP)
    term = first_term(core, first, late_query, passage_tokens, grad_pre)
    outgoing = payload(
        core, first, tile, every, query_tokens, passage_tokens, grad_pre, term, received, sums, grad
    )
    incoming = lax.all_to_all(outgoing.reshape(CHIPS, 8, PAY), CHIP_AXES, 0, 0, tiled=True)
    own_out, send_out = outer_terms(core, incoming)
    grad_in = sum_terms(incoming)
    return (scores, grad_in, own_out + lax.ppermute(send_out, "c", SWAP))


def solution(mesh):
    fine = Mesh(mesh.devices.reshape(2, 2, 4, 2, 2, 2), AXES)
    placed = (
        P(AXES, None, None),
        P(AXES),
        P(DP, None),
        P(None, DP),
        P(),
        P(),
        P(),
        P(AXES, None, None),
        P(),
        P(),
    )
    return jax.shard_map(
        body,
        mesh=fine,
        in_specs=placed,
        out_specs=(P(AXES), P(AXES, None), P(AXES, None)),
        check_vma=False,
    )
```

profile of v0, /device:TPU:1, one launch (start us, length us, event | category | flops | bytes accessed | tf_op | source)
XLA Modules:
  0.0 135.5 jit_solution(5607231052340263997)
XLA Ops:
  0.7 1.0 pack_weights.1
  1.7 1.5 %collective-permute-start = (bf16[1,16,1024]{2,1,0:T(8,128)(2,1)S(1)}, bf16[1,16,1024]{2,1,0:T(8,128)(2,1)S(1)}, u32[]{:S(2)}, u32[]{:S(2)}) collective-permute-start(bf16[1,16,1024]{2,1,0:T(8,128)(2,1)S(1)} %get-tuple-element.68), channel_id=1, source_target_pairs={{0,1},{1,0},{2,3},{3,2},{4,5},{5,4},{6,7},{7,6},{8,9},{9,8},{10,11... | collective-permute-start | bytes 98312 | tf_op jit(solution)/shard_map/ppermute | solution.py:589
  3.2 1.7 %collective-permute-start.1 = (bf16[1,16,1024]{2,1,0:T(8,128)(2,1)S(1)}, bf16[1,16,1024]{2,1,0:T(8,128)(2,1)S(1)}, u32[]{:S(2)}, u32[]{:S(2)}) collective-permute-start(bf16[1,16,1024]{2,1,0:T(8,128)(2,1)S(1)} %get-tuple-element.70), channel_id=1, source_target_pairs={{0,32},{32,0},{1,33},{33,1},{2,34},{34,2},{3,35},{35,3},{4,36},{36... | collective-permute-start | bytes 98312 | tf_op jit(solution)/shard_map/ppermute | solution.py:590
  5.0 0.7 or_bitcast_fusion
  5.7 1.3 pad_maximum_fusion.x0
  7.1 1.2 collective-permute-done.2
  9.2 1.2 collective-permute-start.3
  10.4 1.5 %collective-permute-start.4 = (bf16[2,1,1,32,1024]{4,3,2,0,1:T(8,128)(2,1)S(1)}, bf16[2,1,1,32,1024]{4,3,2,0,1:T(8,128)(2,1)S(1)}, u32[]{:S(2)}, u32[]{:S(2)}) collective-permute-start(bf16[2,1,1,32,1024]{4,3,2,0,1:T(8,128)(2,1)S(1)} %bitcast.26), channel_id=1, source_target_pairs={{0,6},{2,0},{4,2},{6,4},{1,7},{3,1},{5,3},{7,5},{8,14},{10,8},{12,... | collective-permute-start | bytes 393224 | tf_op jit(solution)/shard_map/ppermute | solution.py:58
  11.8 1.5 %collective-permute-start.5 = (bf16[2,1,1,32,1024]{4,3,2,0,1:T(8,128)(2,1)S(1)}, bf16[2,1,1,32,1024]{4,3,2,0,1:T(8,128)(2,1)S(1)}, u32[]{:S(2)}, u32[]{:S(2)}) collective-permute-start(bf16[2,1,1,32,1024]{4,3,2,0,1:T(8,128)(2,1)S(1)} %bitcast.27), channel_id=1, source_target_pairs={{0,4},{2,6},{4,0},{6,2},{1,5},{3,7},{5,1},{7,3},{8,12},{10,14},{12... | collective-permute-start | bytes 393224 | tf_op jit(solution)/shard_map/ppermute | solution.py:58
  13.4 1.5 %collective-permute-done.3 = bf16[2,1,1,32,1024]{4,3,2,0,1:T(8,128)(2,1)S(1)} collective-permute-done((bf16[2,1,1,32,1024]{4,3,2,0,1:T(8,128)(2,1)S(1)}, bf16[2,1,1,32,1024]{4,3,2,0,1:T(8,128)(2,1)S(1)}, u32[]{:S(2)}, u32[]{:S(2)}) %collective-permute-start.3) | collective-permute-done | bytes 131104 | tf_op jit(solution)/shard_map/ppermute | solution.py:58
  15.0 3.8 %collective-permute-done.5 = bf16[2,1,1,32,1024]{4,3,2,0,1:T(8,128)(2,1)S(1)} collective-permute-done((bf16[2,1,1,32,1024]{4,3,2,0,1:T(8,128)(2,1)S(1)}, bf16[2,1,1,32,1024]{4,3,2,0,1:T(8,128)(2,1)S(1)}, u32[]{:S(2)}, u32[]{:S(2)}) %collective-permute-start.5) | collective-permute-done | bytes 131104 | tf_op jit(solution)/shard_map/ppermute | solution.py:58
  18.9 1.4 %collective-permute-start.7 = (bf16[2,1,4,32,1024]{4,3,2,0,1:T(8,128)(2,1)S(1)}, bf16[2,1,4,32,1024]{4,3,2,0,1:T(8,128)(2,1)S(1)}, u32[]{:S(2)}, u32[]{:S(2)}) collective-permute-start(bf16[2,1,4,32,1024]{4,3,2,0,1:T(8,128)(2,1)S(1)} %constant_dynamic-update-slice_fusion), channel_id=1, source_target_pairs={{0,8},{8,16},{16,24},{24,0},{1,9},{9,17},{17,25},{25,1},{2,10},{10... | collective-permute-start | bytes 1572872 | tf_op jit(solution)/shard_map/ppermute | solution.py:58
  20.2 1.5 %collective-permute-start.8 = (bf16[2,1,4,32,1024]{4,3,2,0,1:T(8,128)(2,1)S(1)}, bf16[2,1,4,32,1024]{4,3,2,0,1:T(8,128)(2,1)}, u32[]{:S(2)}, u32[]{:S(2)}) collective-permute-start(bf16[2,1,4,32,1024]{4,3,2,0,1:T(8,128)(2,1)S(1)} %constant_dynamic-update-slice_fusion), channel_id=1, source_target_pairs={{0,24},{8,0},{16,8},{24,16},{1,25},{9,1},{17,9},{25,17},{2,26},{10... | collective-permute-start | bytes 1572872 | tf_op jit(solution)/shard_map/ppermute | solution.py:58
  21.8 1.6 %collective-permute-start.9 = (bf16[2,1,4,32,1024]{4,3,2,0,1:T(8,128)(2,1)S(1)}, bf16[2,1,4,32,1024]{4,3,2,0,1:T(8,128)(2,1)}, u32[]{:S(2)}, u32[]{:S(2)}) collective-permute-start(bf16[2,1,4,32,1024]{4,3,2,0,1:T(8,128)(2,1)S(1)} %constant_dynamic-update-slice_fusion), channel_id=1, source_target_pairs={{0,16},{8,24},{16,0},{24,8},{1,17},{9,25},{17,1},{25,9},{2,18},{10... | collective-permute-start | bytes 1572872 | tf_op jit(solution)/shard_map/ppermute | solution.py:58
  23.3 21.5 %student.1 = (f32[64,4,128]{2,1,0:T(4,128)}, f32[8,128]{1,0:T(8,128)}, bf16[4,768]{1,0:T(4,128)(2,1)}, bf16[2,256,3072]{2,1,0:T(8,128)(2,1)}, bf16[2,512,2304]{2,1,0:T(8,128)(2,1)}) custom-call(s32[2]{0:T(128)} %lens.1, s32[1]{0:T(128)} %bitcast.5.half_ref, s32[1]{0:T(128)} %bitcast.6.first_ref, bf16[8,32,768]{2,1,0:T(8,128)(2,1)} %q_ref.3, ...), custom_call_target="tpu_custom_call" | custom-call | flops 1 | bytes 1 | tf_op jit(solution)/shard_map/student/pallas_call | solution.py:185
  44.9 2.2 %collective-permute-start.11 = (bf16[528,1024]{1,0:T(8,128)(2,1)}, bf16[528,1024]{1,0:T(8,128)(2,1)}, u32[]{:S(2)}, u32[]{:S(2)}) collective-permute-start(bf16[528,1024]{1,0:T(8,128)(2,1)} %collective-permute-done.10.x2), channel_id=1, source_target_pairs={{0,1},{1,0},{2,3},{3,2},{4,5},{5,4},{6,7},{7,6},{8,9},{9,8},{10,11... | collective-permute-start | bytes 3244040 | tf_op jit(solution)/shard_map/ppermute | solution.py:631
  47.2 2.7 %collective-permute-done.11.x3 = bf16[528,1024]{1,0:T(8,128)(2,1)} collective-permute-done((bf16[528,1024]{1,0:T(8,128)(2,1)}, bf16[528,1024]{1,0:T(8,128)(2,1)}, u32[]{:S(2)}, u32[]{:S(2)}) %collective-permute-start.11) | collective-permute-done | bytes 1081376 | tf_op jit(solution)/shard_map/ppermute | solution.py:631
  49.9 0.7 copy-done.3
  50.5 5.5 %teacher_partial.1 = (f32[8,1152]{1,0:T(8,128)S(1)}, f32[8,1152]{1,0:T(8,128)S(1)}, f32[8,1152]{1,0:T(8,128)S(1)}, f32[8,1152]{1,0:T(8,128)S(1)}) custom-call(s32[1]{0:T(128)} %bitcast.y_ref, bf16[528,1024]{1,0:T(8,128)(2,1)S(1)} %pad_maximum_fusion.x0, bf16[528,1024]{1,0:T(8,128)(2,1)S(1)} %collective-permute-done.6.x1, ...), custom_call_target="tpu_custom_call" | custom-call | flops 1000000000 | bytes 6000000 | tf_op jit(solution)/shard_map/teacher_partial/pallas_call | solution.py:372
  56.5 0.9 collective-permute-start.13
  57.4 0.9 collective-permute-start.14
  58.3 1.0 collective-permute-done.13.far
  59.3 1.7 %collective-permute-done.14.both = f32[8,1152]{1,0:T(8,128)S(1)} collective-permute-done((f32[8,1152]{1,0:T(8,128)S(1)}, f32[8,1152]{1,0:T(8,128)S(1)}, u32[]{:S(2)}, u32[]{:S(2)}) %collective-permute-start.14) | collective-permute-done | bytes 36896 | tf_op jit(solution)/shard_map/ppermute | solution.py:643
  61.0 0.9 score_tile.1
  62.9 6.1 %all-to-all-start = ((f32[16,8,128]{2,1,0:T(8,128)}), f32[16,8,128]{2,1,0:T(8,128)S(1)}, u32[]{:S(2)}, u32[]{:S(2)}) async-start(f32[16,8,128]{2,1,0:T(8,128)} %get-tuple-element.56), calls=%async_computation | async-start | bytes 131072 | tf_op jit(solution)/shard_map/all_to_all | solution.py:646
  69.1 5.9 %first_term.1.first_hbm = bf16[512,2304]{1,0:T(8,128)(2,1)} custom-call(s32[1]{0:T(128)} %bitcast.13.half_ref.core_ref, s32[1]{0:T(128)} %bitcast.6.first_ref, bf16[8,32,768]{2,1,0:T(8,128)(2,1)} %q_ref.3, bf16[2,224,768]{2,1,0:T(8,128)(2,1)} %p_ref.5, bf16[2,256,3072]{2,1,0:T(8,128)(2,1)} %get-tuple-element.57.gp_hbm), custom_call_target="tpu_custom_call" | custom-call | flops 3000000000 | bytes 4000000 | tf_op jit(solution)/shard_map/first_term/pallas_call | solution.py:277
  75.0 3.0 %all-to-all-done.all_ref = f32[16,8,128]{2,1,0:T(8,128)S(1)} async-done(((f32[16,8,128]{2,1,0:T(8,128)}), f32[16,8,128]{2,1,0:T(8,128)S(1)}, u32[]{:S(2)}, u32[]{:S(2)}) %all-to-all-start) | async-done | bytes 65568 | tf_op jit(solution)/shard_map/all_to_all | solution.py:646
  78.6 7.3 %payload.1 = bf16[512,2816]{1,0:T(8,128)(2,1)} custom-call(s32[1]{0:T(128)} %bitcast.13.half_ref.core_ref, s32[1]{0:T(128)} %bitcast.6.first_ref, f32[8,128]{1,0:T(8,128)} %copy-done, f32[16,8,128]{2,1,0:T(8,128)} %copy-done.4, bf16[8,32,768]{2,1,0:T(8,128)(2,1)} %q_ref.3, bf16[2,224,768]{2,1,0:T(8,128)(2,1)} %p_ref.5, ...), custom_call_target="tpu_custom_call" | custom-call | tf_op jit(solution)/shard_map/payload/pallas_call | solution.py:489
  85.9 45.3 %all_to_all.10.in_ref = bf16[64,8,2816]{2,1,0:T(8,128)(2,1)S(1)} all-to-all(bf16[64,8,2816]{2,1,0:T(8,128)(2,1)} %bitcast.23), channel_id=1, replica_groups=mesh['zh'=2,'zl'=2,'y'=4,'xh'=2,'xl'=2,'c'=2] {'zh','zl','y','xh','xl'}, dimensions={0} | all-to-all | bytes 5767168 | tf_op jit(solution)/shard_map/all_to_all | solution.py:653
  131.6 2.3 %collective-permute-start.16 = (f32[24,768]{1,0:T(8,128)S(1)}, f32[24,768]{1,0:T(8,128)S(1)}, u32[]{:S(2)}, u32[]{:S(2)}) collective-permute-start(f32[24,768]{1,0:T(8,128)S(1)} %get-tuple-element.64), channel_id=1, source_target_pairs={{0,1},{1,0},{2,3},{3,2},{4,5},{5,4},{6,7},{7,6},{8,9},{9,8},{10,11... | collective-permute-start | bytes 221192 | tf_op jit(solution)/shard_map/ppermute | solution.py:656
  133.9 1.0 sum_terms.1
  134.9 0.6 add.73
  (39 shorter events, 3.7 us)
Async XLA Ops:
  1.7 5.4 %collective-permute-start = (bf16[1,16,1024]{2,1,0:T(8,128)(2,1)S(1)}, bf16[1,16,1024]{2,1,0:T(8,128)(2,1)S(1)}, u32[]{:S(2)}, u32[]{:S(2)}) collective-permute-start(bf16[1,16,1024]{2,1,0:T(8,128)(2,1)S(1)} %get-tuple-element.68), channel_id=1, source_target_pairs={{0,1},{1,0},{2,3},{3,2},{4,5},{5,4},{6,7},{7,6},{8,9},{9,8},{10,11... | collective-permute-start | bytes 98312 | tf_op jit(solution)/shard_map/ppermute | solution.py:589
  3.2 3.9 %collective-permute-start.1 = (bf16[1,16,1024]{2,1,0:T(8,128)(2,1)S(1)}, bf16[1,16,1024]{2,1,0:T(8,128)(2,1)S(1)}, u32[]{:S(2)}, u32[]{:S(2)}) collective-permute-start(bf16[1,16,1024]{2,1,0:T(8,128)(2,1)S(1)} %get-tuple-element.70), channel_id=1, source_target_pairs={{0,32},{32,0},{1,33},{33,1},{2,34},{34,2},{3,35},{35,3},{4,36},{36... | collective-permute-start | bytes 98312 | tf_op jit(solution)/shard_map/ppermute | solution.py:590
  4.9 3.4 %collective-permute-start.2 = (bf16[1,16,1024]{2,1,0:T(8,128)(2,1)S(1)}, bf16[1,16,1024]{2,1,0:T(8,128)(2,1)S(1)}, u32[]{:S(2)}, u32[]{:S(2)}) collective-permute-start(bf16[1,16,1024]{2,1,0:T(8,128)(2,1)S(1)} %get-tuple-element.72), channel_id=1, source_target_pairs={{0,33},{1,32},{32,1},{33,0},{2,35},{3,34},{34,3},{35,2},{4,37},{5,... | collective-permute-start | bytes 98312 | tf_op jit(solution)/shard_map/ppermute | solution.py:591
  8.3 10.6 %collective-permute-start.6 = (bf16[528,1024]{1,0:T(8,128)(2,1)S(1)}, bf16[528,1024]{1,0:T(8,128)(2,1)S(1)}, u32[]{:S(2)}, u32[]{:S(2)}) collective-permute-start(bf16[528,1024]{1,0:T(8,128)(2,1)S(1)} %pad_maximum_fusion.x0), channel_id=1, source_target_pairs={{0,1},{1,0},{2,3},{3,2},{4,5},{5,4},{6,7},{7,6},{8,9},{9,8},{10,11... | collective-permute-start | bytes 3244040 | tf_op jit(solution)/shard_map/ppermute | solution.py:621
  8.6 36.2 %collective-permute-start.10 = (bf16[528,1024]{1,0:T(8,128)(2,1)S(1)}, bf16[528,1024]{1,0:T(8,128)(2,1)}, u32[]{:S(2)}, u32[]{:S(2)}) collective-permute-start(bf16[528,1024]{1,0:T(8,128)(2,1)S(1)} %pad_maximum_fusion.x0), channel_id=1, source_target_pairs={{0,32},{32,0},{1,33},{33,1},{2,34},{34,2},{3,35},{35,3},{4,36},{36... | collective-permute-start | bytes 3244040 | tf_op jit(solution)/shard_map/ppermute | solution.py:620
  9.2 5.8 %collective-permute-start.3 = (bf16[2,1,1,32,1024]{4,3,2,0,1:T(8,128)(2,1)S(1)}, bf16[2,1,1,32,1024]{4,3,2,0,1:T(8,128)(2,1)S(1)}, u32[]{:S(2)}, u32[]{:S(2)}) collective-permute-start(bf16[2,1,1,32,1024]{4,3,2,0,1:T(8,128)(2,1)S(1)} %bitcast.25), channel_id=1, source_target_pairs={{0,2},{2,4},{4,6},{6,0},{1,3},{3,5},{5,7},{7,1},{8,10},{10,12},{12... | collective-permute-start | bytes 393224 | tf_op jit(solution)/shard_map/ppermute | solution.py:58
  10.4 4.6 %collective-permute-start.4 = (bf16[2,1,1,32,1024]{4,3,2,0,1:T(8,128)(2,1)S(1)}, bf16[2,1,1,32,1024]{4,3,2,0,1:T(8,128)(2,1)S(1)}, u32[]{:S(2)}, u32[]{:S(2)}) collective-permute-start(bf16[2,1,1,32,1024]{4,3,2,0,1:T(8,128)(2,1)S(1)} %bitcast.26), channel_id=1, source_target_pairs={{0,6},{2,0},{4,2},{6,4},{1,7},{3,1},{5,3},{7,5},{8,14},{10,8},{12,... | collective-permute-start | bytes 393224 | tf_op jit(solution)/shard_map/ppermute | solution.py:58
  11.8 7.0 %collective-permute-start.5 = (bf16[2,1,1,32,1024]{4,3,2,0,1:T(8,128)(2,1)S(1)}, bf16[2,1,1,32,1024]{4,3,2,0,1:T(8,128)(2,1)S(1)}, u32[]{:S(2)}, u32[]{:S(2)}) collective-permute-start(bf16[2,1,1,32,1024]{4,3,2,0,1:T(8,128)(2,1)S(1)} %bitcast.27), channel_id=1, source_target_pairs={{0,4},{2,6},{4,0},{6,2},{1,5},{3,7},{5,1},{7,3},{8,12},{10,14},{12... | collective-permute-start | bytes 393224 | tf_op jit(solution)/shard_map/ppermute | solution.py:58
  18.9 25.9 %collective-permute-start.7 = (bf16[2,1,4,32,1024]{4,3,2,0,1:T(8,128)(2,1)S(1)}, bf16[2,1,4,32,1024]{4,3,2,0,1:T(8,128)(2,1)S(1)}, u32[]{:S(2)}, u32[]{:S(2)}) collective-permute-start(bf16[2,1,4,32,1024]{4,3,2,0,1:T(8,128)(2,1)S(1)} %constant_dynamic-update-slice_fusion), channel_id=1, source_target_pairs={{0,8},{8,16},{16,24},{24,0},{1,9},{9,17},{17,25},{25,1},{2,10},{10... | collective-permute-start | bytes 1572872 | tf_op jit(solution)/shard_map/ppermute | solution.py:58
  20.2 24.6 %collective-permute-start.8 = (bf16[2,1,4,32,1024]{4,3,2,0,1:T(8,128)(2,1)S(1)}, bf16[2,1,4,32,1024]{4,3,2,0,1:T(8,128)(2,1)}, u32[]{:S(2)}, u32[]{:S(2)}) collective-permute-start(bf16[2,1,4,32,1024]{4,3,2,0,1:T(8,128)(2,1)S(1)} %constant_dynamic-update-slice_fusion), channel_id=1, source_target_pairs={{0,24},{8,0},{16,8},{24,16},{1,25},{9,1},{17,9},{25,17},{2,26},{10... | collective-permute-start | bytes 1572872 | tf_op jit(solution)/shard_map/ppermute | solution.py:58
  21.8 23.2 %collective-permute-start.9 = (bf16[2,1,4,32,1024]{4,3,2,0,1:T(8,128)(2,1)S(1)}, bf16[2,1,4,32,1024]{4,3,2,0,1:T(8,128)(2,1)}, u32[]{:S(2)}, u32[]{:S(2)}) collective-permute-start(bf16[2,1,4,32,1024]{4,3,2,0,1:T(8,128)(2,1)S(1)} %constant_dynamic-update-slice_fusion), channel_id=1, source_target_pairs={{0,16},{8,24},{16,0},{24,8},{1,17},{9,25},{17,1},{25,9},{2,18},{10... | collective-permute-start | bytes 1572872 | tf_op jit(solution)/shard_map/ppermute | solution.py:58
  44.9 4.9 %collective-permute-start.11 = (bf16[528,1024]{1,0:T(8,128)(2,1)}, bf16[528,1024]{1,0:T(8,128)(2,1)}, u32[]{:S(2)}, u32[]{:S(2)}) collective-permute-start(bf16[528,1024]{1,0:T(8,128)(2,1)} %collective-permute-done.10.x2), channel_id=1, source_target_pairs={{0,1},{1,0},{2,3},{3,2},{4,5},{5,4},{6,7},{7,6},{8,9},{9,8},{10,11... | collective-permute-start | bytes 3244040 | tf_op jit(solution)/shard_map/ppermute | solution.py:631
  49.9 0.7 copy-start.3
  50.5 10.5 %copy-start.1 = (f32[1024]{0:T(1024)S(1)}, f32[1024]{0:T(1024)}, u32[]{:S(2)}) copy-start(f32[1024]{0:T(1024)} %param.14) | copy-start | bytes 12292
  50.5 10.5 %copy-start.2 = (f32[1024]{0:T(1024)S(1)}, f32[1024]{0:T(1024)}, u32[]{:S(2)}) copy-start(f32[1024]{0:T(1024)} %param.15) | copy-start | bytes 12292
  56.1 2.2 %collective-permute-start.12 = (f32[8,1152]{1,0:T(8,128)S(1)}, f32[8,1152]{1,0:T(8,128)S(1)}, u32[]{:S(2)}, u32[]{:S(2)}) collective-permute-start(f32[8,1152]{1,0:T(8,128)S(1)} %get-tuple-element.51), channel_id=1, source_target_pairs={{0,1},{1,0},{2,3},{3,2},{4,5},{5,4},{6,7},{7,6},{8,9},{9,8},{10,11... | collective-permute-start | bytes 110600 | tf_op jit(solution)/shard_map/ppermute | solution.py:641
  56.5 2.8 %collective-permute-start.13 = (f32[8,1152]{1,0:T(8,128)S(1)}, f32[8,1152]{1,0:T(8,128)S(1)}, u32[]{:S(2)}, u32[]{:S(2)}) collective-permute-start(f32[8,1152]{1,0:T(8,128)S(1)} %get-tuple-element.52), channel_id=1, source_target_pairs={{0,32},{32,0},{1,33},{33,1},{2,34},{34,2},{3,35},{35,3},{4,36},{36... | collective-permute-start | bytes 110600 | tf_op jit(solution)/shard_map/ppermute | solution.py:642
  57.4 3.6 %collective-permute-start.14 = (f32[8,1152]{1,0:T(8,128)S(1)}, f32[8,1152]{1,0:T(8,128)S(1)}, u32[]{:S(2)}, u32[]{:S(2)}) collective-permute-start(f32[8,1152]{1,0:T(8,128)S(1)} %get-tuple-element.53), channel_id=1, source_target_pairs={{0,33},{1,32},{32,1},{33,0},{2,35},{3,34},{34,3},{35,2},{4,37},{5,... | collective-permute-start | bytes 110600 | tf_op jit(solution)/shard_map/ppermute | solution.py:643
  61.9 0.6 copy-start
  62.5 15.5 %collective-permute-start.15 = (bf16[2,512,2304]{2,1,0:T(8,128)(2,1)}, bf16[2,512,2304]{2,1,0:T(8,128)(2,1)}, u32[]{:S(2)}, u32[]{:S(2)}) collective-permute-start(bf16[2,512,2304]{2,1,0:T(8,128)(2,1)} %get-tuple-element.60), channel_id=1, source_target_pairs={{0,1},{1,0},{2,3},{3,2},{4,5},{5,4},{6,7},{7,6},{8,9},{9,8},{10,11... | collective-permute-start | bytes 14155784 | tf_op jit(solution)/shard_map/ppermute | solution.py:648
  62.9 15.1 %all-to-all-start = ((f32[16,8,128]{2,1,0:T(8,128)}), f32[16,8,128]{2,1,0:T(8,128)S(1)}, u32[]{:S(2)}, u32[]{:S(2)}) async-start(f32[16,8,128]{2,1,0:T(8,128)} %get-tuple-element.56), calls=%async_computation | async-start | bytes 131072 | tf_op jit(solution)/shard_map/all_to_all | solution.py:646
  78.0 0.6 copy-start.4
  131.6 3.3 %collective-permute-start.16 = (f32[24,768]{1,0:T(8,128)S(1)}, f32[24,768]{1,0:T(8,128)S(1)}, u32[]{:S(2)}, u32[]{:S(2)}) collective-permute-start(f32[24,768]{1,0:T(8,128)S(1)} %get-tuple-element.64), channel_id=1, source_target_pairs={{0,1},{1,0},{2,3},{3,2},{4,5},{5,4},{6,7},{7,6},{8,9},{9,8},{10,11... | collective-permute-start | bytes 221192 | tf_op jit(solution)/shard_map/ppermute | solution.py:656
where the time goes:
time: 136 us
  blocking collectives  45.3 us (33%)
  Pallas kernels  42.5 us (31%)
  starting transfers between devices  26.1 us (19%)
  waiting for transfers between devices  15 us (11%)
  local copies, waits for them, and re-layouts  3.04 us (2%)
  other arithmetic  2.68 us (2%)
    all_to_all x1, blocking collectives, body(): lax.all_to_all(outgoing.reshape(CHIPS, 8, PAY), CHIP_AXES, 0, 0, tiled=True)  45.3 us
    pallas_call x1, Pallas kernels, student(): pl.pallas_call(student_kernel, out_shape=(jax.ShapeDtypeStruct((CHIPS, 4,...  21.5 us
    ppermute x6, starting transfers between devices, send_axis(): lax.ppermute(piece, axis, ring(step))  8.66 us
    pallas_call x1, Pallas kernels, payload(): pl.pallas_call(payload_kernel, out_shape=jax.ShapeDtypeStruct((CHIPS * 8,...  7.28 us
    all_to_all x1, starting transfers between devices, body(): every = lax.all_to_all(spread, RIVALS, 0, 0, tiled=True)  6.14 us
    pallas_call x1, Pallas kernels, first_term(): pl.pallas_call(first_kernel, out_shape=jax.ShapeDtypeStruct((8 * CHIPS, W...  5.94 us
    pallas_call x1, Pallas kernels, teacher_partial(): pl.pallas_call(teacher_kernel, out_shape=(shape,) * 4, in_specs=[pl.Block...  5.53 us
    ppermute x6, waiting for transfers between devices, send_axis(): lax.ppermute(piece, axis, ring(step))  5.47 us
  transfers between devices with their start and end apart: 18, of which 8 were waited for; matrix products, arithmetic and copies ran while one was open for 2% of the time, Pallas kernels for 21%

commit v1 on v0

--- a/solution.py
+++ b/solution.py
@@ -152,9 +152,9 @@
     score_ref[...] = jnp.broadcast_to(jnp.concatenate([pairs] * 4, 0), (8, 128))
     grad8 = jnp.concatenate([grad, jnp.zeros((4, DS), BF16)], 0)
     pulled_ref[...] = mm_nt(grad8, wout[...])
-    def backward(j, carry):
+    def backward(j):
         for part in range(3):
-            cols = pl.ds(pl.multiple_of(j * DS + part * 256, 256), 256)
+            cols = slice(j * DS + part * 256, j * DS + part * 256 + 256)
             pulled = pulled_ref[:, cols]
             for i in range(2):
                 gate = jnp.where(at_row < lens[i], pulled[2 * i + 1 : 2 * i + 2], 0.0)
@@ -163,15 +163,20 @@
                     pulled[2 * i : 2 * i + 1] * slope[i * S : i * S + SQ, cols]
                 ).astype(BF16)
         save(j).start()
-        return carry
-
-    lax.fori_loop(0, FF // DS, backward, 0)
+
+    backward(3)
+    backward(0)
     fill = jnp.zeros((4, 16), F32)
     for d in range(CHIPS):
         part = sums[:4, d * 48 : d * 48 + 48]
         sums_tiles[d] = jnp.concatenate([part, fill, part, fill], 1)
     grad_blocks(
-        half_ref[0], rows, gp, blocks, lambda i, k: send(i, k).start()
+        half_ref[0],
+        rows,
+        gp,
+        blocks,
+        ahead=lambda k: backward(k + 1) if k < 2 else None,
+        done=lambda i, k: send(i, k).start(),
     )
     for j in range(FF // DS):
         save(j).wait()
@@ -229,17 +234,18 @@
     ).astype(BF16)
 
 
-def grad_blocks(half, rows, grad, out, done):
-    for i in range(2):
-        wide = select_features(half, rows[i * S : (i + 1) * S])
-        main = wide.astype(BF16)
-        for k in range(3):
-            rest = late_features(wide, k)
+def grad_blocks(half, rows, grad, out, ahead, done):
+    wide = [select_features(half, rows[i * S : (i + 1) * S]) for i in range(2)]
+    main = [values.astype(BF16) for values in wide]
+    for k in range(3):
+        ahead(k)
+        for i in range(2):
+            rest = late_features(wide[i], k)
             for part in range(3):
                 at = k * DS + part * 256
                 late = 3 * DS + part * 256
                 out[i, :, at : at + 256] = (
-                    mm(main, grad[i, :, at : at + 256]) + mm(rest, grad[i, :, late : late + 256])
+                    mm(main[i], grad[i, :, at : at + 256]) + mm(rest, grad[i, :, late : late + 256])
                 ).astype(BF16)
             done(i, k)
 

time: 136 us -> 136 us (level)
  Pallas kernels: 42.5 us -> 41 us
  waiting for transfers between devices: 15 us -> 16.5 us
    pallas_call x1, Pallas kernels: 21.5 us -> 20 us  [student(): pl.pallas_call(student_kernel, out_shape=(jax.ShapeDtypeStruct((CHIPS, 4,...]
    ppermute x6, waiting for transfers between devices: 5.47 us -> 6.98 us  [send_axis(): lax.ppermute(piece, axis, ring(step))]
  transfers between devices with their start and end apart: 18 -> 18, of which waited for: 8 -> 8; matrix products, arithmetic and copies ran while one was open for 2% -> 2% of each run, Pallas kernels for 21% -> 20%
where the time goes in v1:
time: 136 us; the launch traced here: 135 us
  blocking collectives  45.3 us (33%)
  Pallas kernels  41 us (30%)
  starting transfers between devices  25.8 us (19%)
  waiting for transfers between devices  16.5 us (12%)
  local copies, waits for them, and re-layouts  3.04 us (2%)
  other arithmetic  2.68 us (2%)
    all_to_all x1, blocking collectives, body(): lax.all_to_all(outgoing.reshape(CHIPS, 8, PAY), CHIP_AXES, 0, 0, tiled=True)  45.3 us
    pallas_call x1, Pallas kernels, student(): pl.pallas_call(student_kernel, out_shape=(jax.ShapeDtypeStruct((CHIPS, 4,...  20 us
    ppermute x6, starting transfers between devices, send_axis(): lax.ppermute(piece, axis, ring(step))  8.66 us
    pallas_call x1, Pallas kernels, payload(): pl.pallas_call(payload_kernel, out_shape=jax.ShapeDtypeStruct((CHIPS * 8,...  7.28 us
    ppermute x6, waiting for transfers between devices, send_axis(): lax.ppermute(piece, axis, ring(step))  6.98 us
    all_to_all x1, starting transfers between devices, body(): every = lax.all_to_all(spread, RIVALS, 0, 0, tiled=True)  5.97 us
    pallas_call x1, Pallas kernels, first_term(): pl.pallas_call(first_kernel, out_shape=jax.ShapeDtypeStruct((8 * CHIPS, W...  5.94 us
    pallas_call x1, Pallas kernels, teacher_partial(): pl.pallas_call(teacher_kernel, out_shape=(shape,) * 4, in_specs=[pl.Block...  5.53 us
  transfers between devices with their start and end apart: 18, of which 8 were waited for; matrix products, arithmetic and copies ran while one was open for 2% of the time, Pallas kernels for 20%

profile of v1, /device:TPU:1, one launch (start us, length us, event | category | flops | bytes accessed | tf_op | source)
XLA Modules:
  0.0 135.2 jit_solution(2296993591321083891)
XLA Ops:
  0.7 1.0 pack_weights.1
  1.7 1.5 %collective-permute-start = (bf16[1,16,1024]{2,1,0:T(8,128)(2,1)S(1)}, bf16[1,16,1024]{2,1,0:T(8,128)(2,1)S(1)}, u32[]{:S(2)}, u32[]{:S(2)}) collective-permute-start(bf16[1,16,1024]{2,1,0:T(8,128)(2,1)S(1)} %get-tuple-element.68), channel_id=1, source_target_pairs={{0,1},{1,0},{2,3},{3,2},{4,5},{5,4},{6,7},{7,6},{8,9},{9,8},{10,11... | collective-permute-start | bytes 98312 | tf_op jit(solution)/shard_map/ppermute | solution.py:595
  3.2 1.7 %collective-permute-start.1 = (bf16[1,16,1024]{2,1,0:T(8,128)(2,1)S(1)}, bf16[1,16,1024]{2,1,0:T(8,128)(2,1)S(1)}, u32[]{:S(2)}, u32[]{:S(2)}) collective-permute-start(bf16[1,16,1024]{2,1,0:T(8,128)(2,1)S(1)} %get-tuple-element.70), channel_id=1, source_target_pairs={{0,32},{32,0},{1,33},{33,1},{2,34},{34,2},{3,35},{35,3},{4,36},{36... | collective-permute-start | bytes 98312 | tf_op jit(solution)/shard_map/ppermute | solution.py:596
  5.0 0.7 or_bitcast_fusion
  5.7 1.3 pad_maximum_fusion.x0
  7.1 1.2 collective-permute-done.2
  9.2 1.2 collective-permute-start.3
  10.4 1.5 %collective-permute-start.4 = (bf16[2,1,1,32,1024]{4,3,2,0,1:T(8,128)(2,1)S(1)}, bf16[2,1,1,32,1024]{4,3,2,0,1:T(8,128)(2,1)S(1)}, u32[]{:S(2)}, u32[]{:S(2)}) collective-permute-start(bf16[2,1,1,32,1024]{4,3,2,0,1:T(8,128)(2,1)S(1)} %bitcast.26), channel_id=1, source_target_pairs={{0,6},{2,0},{4,2},{6,4},{1,7},{3,1},{5,3},{7,5},{8,14},{10,8},{12,... | collective-permute-start | bytes 393224 | tf_op jit(solution)/shard_map/ppermute | solution.py:58
  11.8 1.5 %collective-permute-start.5 = (bf16[2,1,1,32,1024]{4,3,2,0,1:T(8,128)(2,1)S(1)}, bf16[2,1,1,32,1024]{4,3,2,0,1:T(8,128)(2,1)S(1)}, u32[]{:S(2)}, u32[]{:S(2)}) collective-permute-start(bf16[2,1,1,32,1024]{4,3,2,0,1:T(8,128)(2,1)S(1)} %bitcast.27), channel_id=1, source_target_pairs={{0,4},{2,6},{4,0},{6,2},{1,5},{3,7},{5,1},{7,3},{8,12},{10,14},{12... | collective-permute-start | bytes 393224 | tf_op jit(solution)/shard_map/ppermute | solution.py:58
  13.4 1.5 %collective-permute-done.3 = bf16[2,1,1,32,1024]{4,3,2,0,1:T(8,128)(2,1)S(1)} collective-permute-done((bf16[2,1,1,32,1024]{4,3,2,0,1:T(8,128)(2,1)S(1)}, bf16[2,1,1,32,1024]{4,3,2,0,1:T(8,128)(2,1)S(1)}, u32[]{:S(2)}, u32[]{:S(2)}) %collective-permute-start.3) | collective-permute-done | bytes 131104 | tf_op jit(solution)/shard_map/ppermute | solution.py:58
  15.0 3.8 %collective-permute-done.5 = bf16[2,1,1,32,1024]{4,3,2,0,1:T(8,128)(2,1)S(1)} collective-permute-done((bf16[2,1,1,32,1024]{4,3,2,0,1:T(8,128)(2,1)S(1)}, bf16[2,1,1,32,1024]{4,3,2,0,1:T(8,128)(2,1)S(1)}, u32[]{:S(2)}, u32[]{:S(2)}) %collective-permute-start.5) | collective-permute-done | bytes 131104 | tf_op jit(solution)/shard_map/ppermute | solution.py:58
  18.9 1.4 %collective-permute-start.7 = (bf16[2,1,4,32,1024]{4,3,2,0,1:T(8,128)(2,1)S(1)}, bf16[2,1,4,32,1024]{4,3,2,0,1:T(8,128)(2,1)S(1)}, u32[]{:S(2)}, u32[]{:S(2)}) collective-permute-start(bf16[2,1,4,32,1024]{4,3,2,0,1:T(8,128)(2,1)S(1)} %constant_dynamic-update-slice_fusion), channel_id=1, source_target_pairs={{0,8},{8,16},{16,24},{24,0},{1,9},{9,17},{17,25},{25,1},{2,10},{10... | collective-permute-start | bytes 1572872 | tf_op jit(solution)/shard_map/ppermute | solution.py:58
  20.2 1.5 %collective-permute-start.8 = (bf16[2,1,4,32,1024]{4,3,2,0,1:T(8,128)(2,1)S(1)}, bf16[2,1,4,32,1024]{4,3,2,0,1:T(8,128)(2,1)}, u32[]{:S(2)}, u32[]{:S(2)}) collective-permute-start(bf16[2,1,4,32,1024]{4,3,2,0,1:T(8,128)(2,1)S(1)} %constant_dynamic-update-slice_fusion), channel_id=1, source_target_pairs={{0,24},{8,0},{16,8},{24,16},{1,25},{9,1},{17,9},{25,17},{2,26},{10... | collective-permute-start | bytes 1572872 | tf_op jit(solution)/shard_map/ppermute | solution.py:58
  21.8 1.6 %collective-permute-start.9 = (bf16[2,1,4,32,1024]{4,3,2,0,1:T(8,128)(2,1)S(1)}, bf16[2,1,4,32,1024]{4,3,2,0,1:T(8,128)(2,1)}, u32[]{:S(2)}, u32[]{:S(2)}) collective-permute-start(bf16[2,1,4,32,1024]{4,3,2,0,1:T(8,128)(2,1)S(1)} %constant_dynamic-update-slice_fusion), channel_id=1, source_target_pairs={{0,16},{8,24},{16,0},{24,8},{1,17},{9,25},{17,1},{25,9},{2,18},{10... | collective-permute-start | bytes 1572872 | tf_op jit(solution)/shard_map/ppermute | solution.py:58
  23.3 20.0 %student.1 = (f32[64,4,128]{2,1,0:T(4,128)}, f32[8,128]{1,0:T(8,128)}, bf16[4,768]{1,0:T(4,128)(2,1)}, bf16[2,256,3072]{2,1,0:T(8,128)(2,1)}, bf16[2,512,2304]{2,1,0:T(8,128)(2,1)}) custom-call(s32[2]{0:T(128)} %lens.1, s32[1]{0:T(128)} %bitcast.5.half_ref, s32[1]{0:T(128)} %bitcast.6.first_ref, bf16[8,32,768]{2,1,0:T(8,128)(2,1)} %q_ref.3, ...), custom_call_target="tpu_custom_call" | custom-call | flops 1 | bytes 1 | tf_op jit(solution)/shard_map/student/pallas_call | solution.py:190
  43.3 1.6 %collective-permute-done.9 = bf16[2,1,4,32,1024]{4,3,2,0,1:T(8,128)(2,1)} collective-permute-done((bf16[2,1,4,32,1024]{4,3,2,0,1:T(8,128)(2,1)S(1)}, bf16[2,1,4,32,1024]{4,3,2,0,1:T(8,128)(2,1)}, u32[]{:S(2)}, u32[]{:S(2)}) %collective-permute-start.9) | collective-permute-done | bytes 524320 | tf_op jit(solution)/shard_map/ppermute | solution.py:58
  44.9 2.1 %collective-permute-start.11 = (bf16[528,1024]{1,0:T(8,128)(2,1)}, bf16[528,1024]{1,0:T(8,128)(2,1)}, u32[]{:S(2)}, u32[]{:S(2)}) collective-permute-start(bf16[528,1024]{1,0:T(8,128)(2,1)} %collective-permute-done.10.x2), channel_id=1, source_target_pairs={{0,1},{1,0},{2,3},{3,2},{4,5},{5,4},{6,7},{7,6},{8,9},{9,8},{10,11... | collective-permute-start | bytes 3244040 | tf_op jit(solution)/shard_map/ppermute | solution.py:637
  47.1 2.7 %collective-permute-done.11.x3 = bf16[528,1024]{1,0:T(8,128)(2,1)} collective-permute-done((bf16[528,1024]{1,0:T(8,128)(2,1)}, bf16[528,1024]{1,0:T(8,128)(2,1)}, u32[]{:S(2)}, u32[]{:S(2)}) %collective-permute-start.11) | collective-permute-done | bytes 1081376 | tf_op jit(solution)/shard_map/ppermute | solution.py:637
  49.8 0.7 copy-done.3
  50.5 5.5 %teacher_partial.1 = (f32[8,1152]{1,0:T(8,128)S(1)}, f32[8,1152]{1,0:T(8,128)S(1)}, f32[8,1152]{1,0:T(8,128)S(1)}, f32[8,1152]{1,0:T(8,128)S(1)}) custom-call(s32[1]{0:T(128)} %bitcast.y_ref, bf16[528,1024]{1,0:T(8,128)(2,1)S(1)} %pad_maximum_fusion.x0, bf16[528,1024]{1,0:T(8,128)(2,1)S(1)} %collective-permute-done.6.x1, ...), custom_call_target="tpu_custom_call" | custom-call | flops 1000000000 | bytes 6000000 | tf_op jit(solution)/shard_map/teacher_partial/pallas_call | solution.py:378
  56.4 0.9 collective-permute-start.13
  57.4 0.9 collective-permute-start.14
  58.2 1.0 collective-permute-done.13.far
  59.3 1.7 %collective-permute-done.14.both = f32[8,1152]{1,0:T(8,128)S(1)} collective-permute-done((f32[8,1152]{1,0:T(8,128)S(1)}, f32[8,1152]{1,0:T(8,128)S(1)}, u32[]{:S(2)}, u32[]{:S(2)}) %collective-permute-start.14) | collective-permute-done | bytes 36896 | tf_op jit(solution)/shard_map/ppermute | solution.py:649
  60.9 0.9 score_tile.1
  62.8 6.0 %all-to-all-start = ((f32[16,8,128]{2,1,0:T(8,128)}), f32[16,8,128]{2,1,0:T(8,128)S(1)}, u32[]{:S(2)}, u32[]{:S(2)}) async-start(f32[16,8,128]{2,1,0:T(8,128)} %get-tuple-element.56), calls=%async_computation | async-start | bytes 131072 | tf_op jit(solution)/shard_map/all_to_all | solution.py:652
  68.8 5.9 %first_term.1.first_hbm = bf16[512,2304]{1,0:T(8,128)(2,1)} custom-call(s32[1]{0:T(128)} %bitcast.13.half_ref.core_ref, s32[1]{0:T(128)} %bitcast.6.first_ref, bf16[8,32,768]{2,1,0:T(8,128)(2,1)} %q_ref.3, bf16[2,224,768]{2,1,0:T(8,128)(2,1)} %p_ref.5, bf16[2,256,3072]{2,1,0:T(8,128)(2,1)} %get-tuple-element.57.gp_hbm), custom_call_target="tpu_custom_call" | custom-call | flops 3000000000 | bytes 4000000 | tf_op jit(solution)/shard_map/first_term/pallas_call | solution.py:283
  74.8 3.0 %all-to-all-done.all_ref = f32[16,8,128]{2,1,0:T(8,128)S(1)} async-done(((f32[16,8,128]{2,1,0:T(8,128)}), f32[16,8,128]{2,1,0:T(8,128)S(1)}, u32[]{:S(2)}, u32[]{:S(2)}) %all-to-all-start) | async-done | bytes 65568 | tf_op jit(solution)/shard_map/all_to_all | solution.py:652
  78.4 7.3 %payload.1 = bf16[512,2816]{1,0:T(8,128)(2,1)} custom-call(s32[1]{0:T(128)} %bitcast.13.half_ref.core_ref, s32[1]{0:T(128)} %bitcast.6.first_ref, f32[8,128]{1,0:T(8,128)} %copy-done, f32[16,8,128]{2,1,0:T(8,128)} %copy-done.4, bf16[8,32,768]{2,1,0:T(8,128)(2,1)} %q_ref.3, bf16[2,224,768]{2,1,0:T(8,128)(2,1)} %p_ref.5, ...), custom_call_target="tpu_custom_call" | custom-call | tf_op jit(solution)/shard_map/payload/pallas_call | solution.py:495
  85.7 45.3 %all_to_all.10.in_ref = bf16[64,8,2816]{2,1,0:T(8,128)(2,1)S(1)} all-to-all(bf16[64,8,2816]{2,1,0:T(8,128)(2,1)} %bitcast.23), channel_id=1, replica_groups=mesh['zh'=2,'zl'=2,'y'=4,'xh'=2,'xl'=2,'c'=2] {'zh','zl','y','xh','xl'}, dimensions={0} | all-to-all | bytes 5767168 | tf_op jit(solution)/shard_map/all_to_all | solution.py:659
  131.3 2.3 %collective-permute-start.16 = (f32[24,768]{1,0:T(8,128)S(1)}, f32[24,768]{1,0:T(8,128)S(1)}, u32[]{:S(2)}, u32[]{:S(2)}) collective-permute-start(f32[24,768]{1,0:T(8,128)S(1)} %get-tuple-element.64), channel_id=1, source_target_pairs={{0,1},{1,0},{2,3},{3,2},{4,5},{5,4},{6,7},{7,6},{8,9},{9,8},{10,11... | collective-permute-start | bytes 221192 | tf_op jit(solution)/shard_map/ppermute | solution.py:662
  133.6 1.0 sum_terms.1
  (39 shorter events, 4.2 us)
Async XLA Ops:
  1.7 5.4 %collective-permute-start = (bf16[1,16,1024]{2,1,0:T(8,128)(2,1)S(1)}, bf16[1,16,1024]{2,1,0:T(8,128)(2,1)S(1)}, u32[]{:S(2)}, u32[]{:S(2)}) collective-permute-start(bf16[1,16,1024]{2,1,0:T(8,128)(2,1)S(1)} %get-tuple-element.68), channel_id=1, source_target_pairs={{0,1},{1,0},{2,3},{3,2},{4,5},{5,4},{6,7},{7,6},{8,9},{9,8},{10,11... | collective-permute-start | bytes 98312 | tf_op jit(solution)/shard_map/ppermute | solution.py:595
  3.2 3.9 %collective-permute-start.1 = (bf16[1,16,1024]{2,1,0:T(8,128)(2,1)S(1)}, bf16[1,16,1024]{2,1,0:T(8,128)(2,1)S(1)}, u32[]{:S(2)}, u32[]{:S(2)}) collective-permute-start(bf16[1,16,1024]{2,1,0:T(8,128)(2,1)S(1)} %get-tuple-element.70), channel_id=1, source_target_pairs={{0,32},{32,0},{1,33},{33,1},{2,34},{34,2},{3,35},{35,3},{4,36},{36... | collective-permute-start | bytes 98312 | tf_op jit(solution)/shard_map/ppermute | solution.py:596
  4.9 3.4 %collective-permute-start.2 = (bf16[1,16,1024]{2,1,0:T(8,128)(2,1)S(1)}, bf16[1,16,1024]{2,1,0:T(8,128)(2,1)S(1)}, u32[]{:S(2)}, u32[]{:S(2)}) collective-permute-start(bf16[1,16,1024]{2,1,0:T(8,128)(2,1)S(1)} %get-tuple-element.72), channel_id=1, source_target_pairs={{0,33},{1,32},{32,1},{33,0},{2,35},{3,34},{34,3},{35,2},{4,37},{5,... | collective-permute-start | bytes 98312 | tf_op jit(solution)/shard_map/ppermute | solution.py:597
  8.3 10.6 %collective-permute-start.6 = (bf16[528,1024]{1,0:T(8,128)(2,1)S(1)}, bf16[528,1024]{1,0:T(8,128)(2,1)S(1)}, u32[]{:S(2)}, u32[]{:S(2)}) collective-permute-start(bf16[528,1024]{1,0:T(8,128)(2,1)S(1)} %pad_maximum_fusion.x0), channel_id=1, source_target_pairs={{0,1},{1,0},{2,3},{3,2},{4,5},{5,4},{6,7},{7,6},{8,9},{9,8},{10,11... | collective-permute-start | bytes 3244040 | tf_op jit(solution)/shard_map/ppermute | solution.py:627
  8.6 34.7 %collective-permute-start.10 = (bf16[528,1024]{1,0:T(8,128)(2,1)S(1)}, bf16[528,1024]{1,0:T(8,128)(2,1)}, u32[]{:S(2)}, u32[]{:S(2)}) collective-permute-start(bf16[528,1024]{1,0:T(8,128)(2,1)S(1)} %pad_maximum_fusion.x0), channel_id=1, source_target_pairs={{0,32},{32,0},{1,33},{33,1},{2,34},{34,2},{3,35},{35,3},{4,36},{36... | collective-permute-start | bytes 3244040 | tf_op jit(solution)/shard_map/ppermute | solution.py:626
  9.2 5.8 %collective-permute-start.3 = (bf16[2,1,1,32,1024]{4,3,2,0,1:T(8,128)(2,1)S(1)}, bf16[2,1,1,32,1024]{4,3,2,0,1:T(8,128)(2,1)S(1)}, u32[]{:S(2)}, u32[]{:S(2)}) collective-permute-start(bf16[2,1,1,32,1024]{4,3,2,0,1:T(8,128)(2,1)S(1)} %bitcast.25), channel_id=1, source_target_pairs={{0,2},{2,4},{4,6},{6,0},{1,3},{3,5},{5,7},{7,1},{8,10},{10,12},{12... | collective-permute-start | bytes 393224 | tf_op jit(solution)/shard_map/ppermute | solution.py:58
  10.4 4.6 %collective-permute-start.4 = (bf16[2,1,1,32,1024]{4,3,2,0,1:T(8,128)(2,1)S(1)}, bf16[2,1,1,32,1024]{4,3,2,0,1:T(8,128)(2,1)S(1)}, u32[]{:S(2)}, u32[]{:S(2)}) collective-permute-start(bf16[2,1,1,32,1024]{4,3,2,0,1:T(8,128)(2,1)S(1)} %bitcast.26), channel_id=1, source_target_pairs={{0,6},{2,0},{4,2},{6,4},{1,7},{3,1},{5,3},{7,5},{8,14},{10,8},{12,... | collective-permute-start | bytes 393224 | tf_op jit(solution)/shard_map/ppermute | solution.py:58
  11.8 7.0 %collective-permute-start.5 = (bf16[2,1,1,32,1024]{4,3,2,0,1:T(8,128)(2,1)S(1)}, bf16[2,1,1,32,1024]{4,3,2,0,1:T(8,128)(2,1)S(1)}, u32[]{:S(2)}, u32[]{:S(2)}) collective-permute-start(bf16[2,1,1,32,1024]{4,3,2,0,1:T(8,128)(2,1)S(1)} %bitcast.27), channel_id=1, source_target_pairs={{0,4},{2,6},{4,0},{6,2},{1,5},{3,7},{5,1},{7,3},{8,12},{10,14},{12... | collective-permute-start | bytes 393224 | tf_op jit(solution)/shard_map/ppermute | solution.py:58
  18.9 24.4 %collective-permute-start.7 = (bf16[2,1,4,32,1024]{4,3,2,0,1:T(8,128)(2,1)S(1)}, bf16[2,1,4,32,1024]{4,3,2,0,1:T(8,128)(2,1)S(1)}, u32[]{:S(2)}, u32[]{:S(2)}) collective-permute-start(bf16[2,1,4,32,1024]{4,3,2,0,1:T(8,128)(2,1)S(1)} %constant_dynamic-update-slice_fusion), channel_id=1, source_target_pairs={{0,8},{8,16},{16,24},{24,0},{1,9},{9,17},{17,25},{25,1},{2,10},{10... | collective-permute-start | bytes 1572872 | tf_op jit(solution)/shard_map/ppermute | solution.py:58
  20.2 23.1 %collective-permute-start.8 = (bf16[2,1,4,32,1024]{4,3,2,0,1:T(8,128)(2,1)S(1)}, bf16[2,1,4,32,1024]{4,3,2,0,1:T(8,128)(2,1)}, u32[]{:S(2)}, u32[]{:S(2)}) collective-permute-start(bf16[2,1,4,32,1024]{4,3,2,0,1:T(8,128)(2,1)S(1)} %constant_dynamic-update-slice_fusion), channel_id=1, source_target_pairs={{0,24},{8,0},{16,8},{24,16},{1,25},{9,1},{17,9},{25,17},{2,26},{10... | collective-permute-start | bytes 1572872 | tf_op jit(solution)/shard_map/ppermute | solution.py:58
  21.8 23.2 %collective-permute-start.9 = (bf16[2,1,4,32,1024]{4,3,2,0,1:T(8,128)(2,1)S(1)}, bf16[2,1,4,32,1024]{4,3,2,0,1:T(8,128)(2,1)}, u32[]{:S(2)}, u32[]{:S(2)}) collective-permute-start(bf16[2,1,4,32,1024]{4,3,2,0,1:T(8,128)(2,1)S(1)} %constant_dynamic-update-slice_fusion), channel_id=1, source_target_pairs={{0,16},{8,24},{16,0},{24,8},{1,17},{9,25},{17,1},{25,9},{2,18},{10... | collective-permute-start | bytes 1572872 | tf_op jit(solution)/shard_map/ppermute | solution.py:58
  44.9 4.8 %collective-permute-start.11 = (bf16[528,1024]{1,0:T(8,128)(2,1)}, bf16[528,1024]{1,0:T(8,128)(2,1)}, u32[]{:S(2)}, u32[]{:S(2)}) collective-permute-start(bf16[528,1024]{1,0:T(8,128)(2,1)} %collective-permute-done.10.x2), channel_id=1, source_target_pairs={{0,1},{1,0},{2,3},{3,2},{4,5},{5,4},{6,7},{7,6},{8,9},{9,8},{10,11... | collective-permute-start | bytes 3244040 | tf_op jit(solution)/shard_map/ppermute | solution.py:637
  49.8 0.7 copy-start.3
  50.4 10.5 %copy-start.1 = (f32[1024]{0:T(1024)S(1)}, f32[1024]{0:T(1024)}, u32[]{:S(2)}) copy-start(f32[1024]{0:T(1024)} %param.14) | copy-start | bytes 12292
  50.4 10.5 %copy-start.2 = (f32[1024]{0:T(1024)S(1)}, f32[1024]{0:T(1024)}, u32[]{:S(2)}) copy-start(f32[1024]{0:T(1024)} %param.15) | copy-start | bytes 12292
  56.0 2.2 %collective-permute-start.12 = (f32[8,1152]{1,0:T(8,128)S(1)}, f32[8,1152]{1,0:T(8,128)S(1)}, u32[]{:S(2)}, u32[]{:S(2)}) collective-permute-start(f32[8,1152]{1,0:T(8,128)S(1)} %get-tuple-element.51), channel_id=1, source_target_pairs={{0,1},{1,0},{2,3},{3,2},{4,5},{5,4},{6,7},{7,6},{8,9},{9,8},{10,11... | collective-permute-start | bytes 110600 | tf_op jit(solution)/shard_map/ppermute | solution.py:647
  56.4 2.8 %collective-permute-start.13 = (f32[8,1152]{1,0:T(8,128)S(1)}, f32[8,1152]{1,0:T(8,128)S(1)}, u32[]{:S(2)}, u32[]{:S(2)}) collective-permute-start(f32[8,1152]{1,0:T(8,128)S(1)} %get-tuple-element.52), channel_id=1, source_target_pairs={{0,32},{32,0},{1,33},{33,1},{2,34},{34,2},{3,35},{35,3},{4,36},{36... | collective-permute-start | bytes 110600 | tf_op jit(solution)/shard_map/ppermute | solution.py:648
  57.4 3.6 %collective-permute-start.14 = (f32[8,1152]{1,0:T(8,128)S(1)}, f32[8,1152]{1,0:T(8,128)S(1)}, u32[]{:S(2)}, u32[]{:S(2)}) collective-permute-start(f32[8,1152]{1,0:T(8,128)S(1)} %get-tuple-element.53), channel_id=1, source_target_pairs={{0,33},{1,32},{32,1},{33,0},{2,35},{3,34},{34,3},{35,2},{4,37},{5,... | collective-permute-start | bytes 110600 | tf_op jit(solution)/shard_map/ppermute | solution.py:649
  61.9 0.6 copy-start
  62.4 15.3 %collective-permute-start.15 = (bf16[2,512,2304]{2,1,0:T(8,128)(2,1)}, bf16[2,512,2304]{2,1,0:T(8,128)(2,1)}, u32[]{:S(2)}, u32[]{:S(2)}) collective-permute-start(bf16[2,512,2304]{2,1,0:T(8,128)(2,1)} %get-tuple-element.60), channel_id=1, source_target_pairs={{0,1},{1,0},{2,3},{3,2},{4,5},{5,4},{6,7},{7,6},{8,9},{9,8},{10,11... | collective-permute-start | bytes 14155784 | tf_op jit(solution)/shard_map/ppermute | solution.py:654
  62.8 14.9 %all-to-all-start = ((f32[16,8,128]{2,1,0:T(8,128)}), f32[16,8,128]{2,1,0:T(8,128)S(1)}, u32[]{:S(2)}, u32[]{:S(2)}) async-start(f32[16,8,128]{2,1,0:T(8,128)} %get-tuple-element.56), calls=%async_computation | async-start | bytes 131072 | tf_op jit(solution)/shard_map/all_to_all | solution.py:652
  77.7 0.6 copy-start.4
  131.3 3.3 %collective-permute-start.16 = (f32[24,768]{1,0:T(8,128)S(1)}, f32[24,768]{1,0:T(8,128)S(1)}, u32[]{:S(2)}, u32[]{:S(2)}) collective-permute-start(f32[24,768]{1,0:T(8,128)S(1)} %get-tuple-element.64), channel_id=1, source_target_pairs={{0,1},{1,0},{2,3},{3,2},{4,5},{5,4},{6,7},{7,6},{8,9},{9,8},{10,11... | collective-permute-start | bytes 221192 | tf_op jit(solution)/shard_map/ppermute | solution.py:662
